TPU v7x, 256 devices: a whole 4x4x8 slice. The times are simulated.
256 devices in a mesh: ep: 32 (over x, z), tp: 8 (over y, core).
Axes of the slice: x: 4, y: 4, z: 8, core: 2. Of those that a mesh axis runs over, the one named last changes fastest.
Arguments:
- tokens: bfloat16 [4096, 6144], P('ep', 'tp'), may hold values from -6 to 6
- cotangent: bfloat16 [4096, 6144], P('ep', 'tp'), may hold values from -6 to 6
- routes: int32 [4096, 2], P('ep'), may hold values from 0 to 7, all different within a row; in each aligned block of 128 rows (0 to 127, 128 to 255, ...) at most 40 rows name the same one
- route_gates: bfloat16 [4096, 2], P('ep'), may hold values from 0.19921875 to 1
- example_ids: int32 [32, 128], P('ep'), may hold values from 0 to 3, never falling along the last dimension, each value on 1 to 64 neighbouring positions
- gate_weight: bfloat16 [32, 6144, 2048], P('ep', None, 'tp'), may hold values from -2 to 2
- up_weight: bfloat16 [32, 6144, 2048], P('ep', None, 'tp'), may hold values from -2 to 2
Outputs:
- clipped_sum: bfloat16 [32, 2048, 6144], P('ep', None, 'tp')
- norm_ratio: float32 [128], replicated
Inputs may be any that keep to these rules, and one draw needn't show every extreme that they name: `routes`: within the rows of one device (aligned blocks of 128 tokens) no expert is named more than 40 times; the 2 experts of a token differ. example_ids never falls along a row, and each of the 4 examples of a row has 1 to 64 tokens.
All inputs are finite; a program needn't handle non-finite values.
Results may differ from a plain program's by a relative error of at most 0.0012.
The roundings to bfloat16 on the way count: a program that leaves them out, or rounds other values in their place, can miss the bound.
Values may be sent and summed in bfloat16 or wider, within the bound.
A program may use at most 128 MiB of HBM per device.

v0:
```python
import jax
import jax.numpy as jnp
from jax import lax
from jax.sharding import PartitionSpec as P

D = 6144
FF = 8192
EXPERTS = 8
TOPK = 2
EX_DEV = 4
CAP = 40


CLIP_SCALE = 0.6


def slot_table(route_rows, experts, capacity):
    row_count = route_rows.shape[0]
    flat_routes = route_rows.reshape(row_count, -1)
    expert_ids = jnp.arange(experts, dtype=jnp.int32)
    onehot = (flat_routes[:, :, None] == expert_ids[None, None, :]).astype(jnp.int32)
    slot_ranks = jnp.sum((jnp.cumsum(onehot, axis=1) - 1) * onehot, axis=2)
    slot_ids = jnp.arange(capacity, dtype=jnp.int32)
    matches = (flat_routes[:, None, None, :] == expert_ids[None, :, None, None]) & (
        slot_ranks[:, None, None, :] == slot_ids[None, None, :, None]
    )
    matches = matches.astype(jnp.int32)
    positions = jnp.arange(flat_routes.shape[1], dtype=jnp.int32)
    chosen = jnp.sum(matches * positions[None, None, None, :], axis=3)
    valid_mask = jnp.sum(matches, axis=3)
    return (chosen, valid_mask)


def replicate_rows(values, group_size):
    return jnp.repeat(values, group_size, axis=0)


def body(tokens, cotangent, routes, route_gates, example_ids, gate_weight, up_weight):
    ep_count = lax.axis_size("ep")
    group_size = ep_count // EXPERTS
    feature_share = tokens.shape[1]
    unit_count = gate_weight.shape[2]
    clip_level = CLIP_SCALE * (FF * D) ** 0.5
    chosen, valid_mask = slot_table(routes[None], EXPERTS, CAP)
    chosen = chosen[0]
    valid_mask = valid_mask[0]
    token_of = chosen // TOPK
    keep_mask = valid_mask.astype(jnp.bfloat16)
    slot_gate = route_gates.reshape(-1)[chosen] * keep_mask
    slot_example = example_ids[0][token_of]
    c_send = cotangent[token_of] * keep_mask[..., None]
    gate_send = replicate_rows(slot_gate, group_size)
    example_send = replicate_rows(slot_example, group_size)
    token_full = lax.all_gather(tokens, "tp", axis=1, tiled=True)
    x_send = token_full[token_of] * keep_mask[..., None]
    x_recv, c_recv, gate_recv, example_recv = (
        lax.all_to_all(
            replicate_rows(x_send, group_size), "ep", split_axis=0, concat_axis=0, tiled=True
        ),
        lax.all_to_all(
            replicate_rows(c_send, group_size), "ep", split_axis=0, concat_axis=0, tiled=True
        ),
        lax.all_to_all(gate_send, "ep", split_axis=0, concat_axis=0, tiled=True),
        lax.all_to_all(example_send, "ep", split_axis=0, concat_axis=0, tiled=True),
    )
    flat_slots = x_recv.reshape(-1, D)
    gate_sum = jnp.dot(flat_slots, gate_weight[0], preferred_element_type=jnp.float32)
    up_sum = jnp.dot(flat_slots, up_weight[0], preferred_element_type=jnp.float32)
    hidden = (jax.nn.silu(gate_sum) * up_sum).astype(jnp.bfloat16)
    hidden_blocks = hidden.reshape(ep_count, CAP, unit_count)
    hidden_pairs = jnp.einsum(
        "jah,jbh->jab", hidden_blocks, hidden_blocks, preferred_element_type=jnp.float32
    )
    cot_pairs = lax.psum(
        jnp.einsum("jad,jbd->jab", c_recv, c_recv, preferred_element_type=jnp.float32), "tp"
    )
    weights_float = gate_recv.astype(jnp.float32)
    same_example = (example_recv[:, :, None] == example_recv[:, None, :]).astype(jnp.float32)
    pair_terms = (
        weights_float[:, :, None]
        * weights_float[:, None, :]
        * same_example
        * hidden_pairs
        * cot_pairs
    )
    per_slot = jnp.sum(pair_terms, axis=2)
    example_onehot = (
        example_recv[:, :, None] == jnp.arange(EX_DEV, dtype=jnp.int32)[None, None, :]
    ).astype(jnp.float32)
    partial_norms = jnp.sum(per_slot[:, :, None] * example_onehot, axis=1).reshape(-1)
    norm_sq = lax.psum(partial_norms, ("ep", "tp"))
    norm_value = jnp.sqrt(norm_sq)
    norm_ratio = norm_value / clip_level
    factor = clip_level / jnp.maximum(norm_value, clip_level)
    slot_factor = jnp.sum(example_onehot * factor.reshape(ep_count, EX_DEV)[:, None, :], axis=2)
    scaled = (
        ((slot_factor * weights_float)[:, :, None] * c_recv.astype(jnp.float32))
        .astype(jnp.bfloat16)
        .reshape(-1, feature_share)
    )
    update = jnp.einsum(
        "sh,sd->hd",
        lax.all_gather(hidden, "tp", axis=1, tiled=True),
        scaled,
        preferred_element_type=jnp.float32,
    )
    return (update.astype(jnp.bfloat16)[None], norm_ratio)


def solution(mesh):
    placed = (
        P("ep", "tp"),
        P("ep", "tp"),
        P("ep", None),
        P("ep", None),
        P("ep", None),
        P("ep", None, "tp"),
        P("ep", None, "tp"),
    )
    return jax.shard_map(
        body, mesh=mesh, in_specs=placed, out_specs=(P("ep", None, "tp"), P()), check_vma=False
    )
```

profile of v0, /device:TPU:1, one launch (start us, length us, event | category | flops | bytes accessed | tf_op | source)
XLA Modules:
  0.0 625.8 jit_solution(12858374919401784037)
XLA Ops:
  7.2 0.7 all-gather.3.cloned.1.call-update
  7.9 0.9 copy.20
  9.0 0.6 reduce-window.6
  9.9 0.4 fusion.14
  10.5 0.8 copy.21
  11.4 2.4 gather_fusion.2
  13.9 2.6 gather_fusion.3
  16.5 1.1 broadcast_multiply_fusion.1
  17.7 1.4 broadcast_in_dim.13
  19.1 12.0 %all-to-all-start.3 = ((bf16[32,40,768]{2,1,0:T(8,128)(2,1)}), bf16[32,40,768]{2,1,0:T(8,128)(2,1)}, u32[]{:S(2)}, u32[]{:S(2)}) async-start(bf16[32,40,768]{2,1,0:T(8,128)(2,1)} %bitcast.81), calls=%async_computation.3 | async-start | bytes 3932160 | tf_op jit(solution)/shard_map/all_to_all | solution.py:60
  31.0 10.0 %all-gather.3.cloned.1.call-done = bf16[128,6144]{1,0:T(8,128)(2,1)} async-done(((bf16[128,768]{1,0:T(8,128)(2,1)}), bf16[128,6144]{1,0:T(8,128)(2,1)}) %all-gather.3.cloned.1.call-update) | async-done | bytes 1572880 | tf_op jit(solution)/shard_map/all_gather | solution.py:54
  41.0 13.0 %gather_fusion = bf16[320,6144]{1,0:T(8,128)(2,1)} fusion(bf16[128,6144]{1,0:T(8,128)(2,1)} %all-gather.3.cloned.1.call-done, s32[1024]{0:T(1024)S(1)} %pad_clamp_fusion.1), kind=kCustom, calls=%fused_computation | custom fusion | bytes 7865600 | tf_op jit(solution)/shard_map/gather | solution.py:55
  54.0 4.3 broadcast_multiply_fusion
  58.4 18.9 %all-to-all-done.3 = bf16[32,40,768]{2,1,0:T(8,128)(2,1)} async-done(((bf16[32,40,768]{2,1,0:T(8,128)(2,1)}), bf16[32,40,768]{2,1,0:T(8,128)(2,1)}, u32[]{:S(2)}, u32[]{:S(2)}) %all-to-all-start.3) | async-done | bytes 1966112 | tf_op jit(solution)/shard_map/all_to_all | solution.py:60
  77.3 7.1 %broadcast_in_dim.10 = bf16[8,4,40,6144]{3,2,1,0:T(8,128)(2,1)} broadcast(bf16[8,40,6144]{2,1,0:T(8,128)(2,1)} %broadcast_multiply_fusion), dimensions={0,2,3} | broadcast | bytes 19660800 | tf_op jit(solution)/shard_map/broadcast_in_dim | solution.py:35
  84.3 6.8 %all-to-all-start = ((bf16[32,40,6144]{2,1,0:T(8,128)(2,1)}), bf16[32,40,6144]{2,1,0:T(8,128)(2,1)}, u32[]{:S(2)}, u32[]{:S(2)}) async-start(bf16[32,40,6144]{2,1,0:T(8,128)(2,1)} %bitcast.79), calls=%async_computation | async-start | bytes 31457280 | tf_op jit(solution)/shard_map/all_to_all | solution.py:57
  91.2 3.7 fusion.22
  95.2 346.9 %all-to-all-done = bf16[32,40,6144]{2,1,0:T(8,128)(2,1)} async-done(((bf16[32,40,6144]{2,1,0:T(8,128)(2,1)}), bf16[32,40,6144]{2,1,0:T(8,128)(2,1)}, u32[]{:S(2)}, u32[]{:S(2)}) %all-to-all-start) | async-done | bytes 15728672 | tf_op jit(solution)/shard_map/all_to_all | solution.py:57
  442.1 7.8 %fusion.2 = f32[1280,256]{1,0:T(8,128)S(1)} fusion(bf16[1280,6144]{1,0:T(8,128)(2,1)} %bitcast.9, bf16[1,6144,256]{2,1,0:T(8,128)(2,1)S(1)} %copy-done), kind=kOutput, calls=%fused_computation.8 | convolution fusion | flops 4026531840 | bytes 20185088 | tf_op jit(solution)/shard_map/dot_general | solution.py:67
  449.9 8.9 %fusion.8 = bf16[1280,256]{1,0:T(8,128)(2,1)} fusion(bf16[1280,6144]{1,0:T(8,128)(2,1)} %bitcast.9, bf16[1,6144,256]{2,1,0:T(8,128)(2,1)S(1)} %copy-done.3, f32[1280,256]{1,0:T(8,128)S(1)} %fusion.2), kind=kOutput, calls=%fused_computation.12 | convolution fusion | flops 4028497920 | bytes 20840448 | tf_op jit(solution)/shard_map/dot_general | solution.py:68
  458.9 0.6 copy.22
  459.5 46.0 %all-to-all-start.2 = ((bf16[32,1,40]{2,1,0:T(2,128)(2,1)}), bf16[32,1,40]{2,1,0:T(2,128)(2,1)S(1)}, u32[]{:S(2)}, u32[]{:S(2)}) async-start(bf16[32,1,40]{2,1,0:T(2,128)(2,1)} %copy.22), calls=%async_computation.2 | async-start | bytes 32768 | tf_op jit(solution)/shard_map/all_to_all | solution.py:63
  505.6 2.4 gather_fusion.1
  508.0 6.2 all-to-all-done.2
  514.2 0.6 broadcast_in_dim.11
  514.8 3.8 all-to-all-start.1
  518.6 8.6 %all-to-all-done.1 = s32[32,1,40]{2,1,0:T(1,128)S(1)} async-done(((s32[32,1,40]{2,1,0:T(1,128)}), s32[32,1,40]{2,1,0:T(1,128)S(1)}, u32[]{:S(2)}, u32[]{:S(2)}) %all-to-all-start.1) | async-done | bytes 5152 | tf_op jit(solution)/shard_map/all_to_all | solution.py:64
  527.2 2.0 fusion.12
  529.5 76.6 %psum.15 = f32[128]{0:T(128)S(1)} all-reduce(f32[128]{0:T(128)S(1)} %reshape.328), channel_id=1, replica_groups=mesh['ep'=32,'tp'=8] {'ep','tp'}, use_global_device_ids=true, to_apply=%region_8.9 | all-reduce | flops 128 | bytes 1024 | tf_op jit(solution)/shard_map/psum | solution.py:91
  606.1 0.5 sqrt_multiply_fusion
  606.9 3.3 multiply_convert_fusion
  610.2 9.1 %fusion.4 = bf16[1,2048,768]{2,1,0:T(8,128)(2,1)} fusion(bf16[1280,2048]{1,0:T(8,128)(2,1)} %all-gather.5.cloned.1.call-done, bf16[1280,768]{1,0:T(8,128)(2,1)} %bitcast.82), kind=kOutput, calls=%fused_computation.10 | convolution fusion | flops 4028104704 | bytes 10354688 | tf_op jit(solution)/shard_map/sh,sd->hd/dot_general | solution.py:101
  (41 shorter events, 1.9 us)
Async XLA Ops:
  7.2 434.9 %copy-start = (bf16[1,6144,256]{2,1,0:T(8,128)(2,1)S(1)}, bf16[1,6144,256]{2,1,0:T(8,128)(2,1)}, u32[]{:S(2)}) copy-start(bf16[1,6144,256]{2,1,0:T(8,128)(2,1)} %param.12) | copy-start | bytes 9437188
  7.2 6.7 %copy-start.2 = (bf16[128,768]{1,0:T(8,128)(2,1)S(1)}, bf16[128,768]{1,0:T(8,128)(2,1)}, u32[]{:S(2)}) copy-start(bf16[128,768]{1,0:T(8,128)(2,1)} %param.8) | copy-start | bytes 589828
  7.2 33.8 %all-gather.3.cloned.1.call-start = ((), (), s32[]{:S(2)}) async-start(), calls=%async_computation.4 | async-start | bytes 1769472 | tf_op jit(solution)/shard_map/all_gather | solution.py:54
  19.1 58.2 %all-to-all-start.3 = ((bf16[32,40,768]{2,1,0:T(8,128)(2,1)}), bf16[32,40,768]{2,1,0:T(8,128)(2,1)}, u32[]{:S(2)}, u32[]{:S(2)}) async-start(bf16[32,40,768]{2,1,0:T(8,128)(2,1)} %bitcast.81), calls=%async_computation.3 | async-start | bytes 3932160 | tf_op jit(solution)/shard_map/all_to_all | solution.py:60
  84.3 357.7 %all-to-all-start = ((bf16[32,40,6144]{2,1,0:T(8,128)(2,1)}), bf16[32,40,6144]{2,1,0:T(8,128)(2,1)}, u32[]{:S(2)}, u32[]{:S(2)}) async-start(bf16[32,40,6144]{2,1,0:T(8,128)(2,1)} %bitcast.79), calls=%async_computation | async-start | bytes 31457280 | tf_op jit(solution)/shard_map/all_to_all | solution.py:57
  91.2 436.1 %all-reduce.2.cloned.1.call-start = ((), (), s32[]{:S(2)}) async-start(), calls=%async_computation.6 | async-start | bytes 1310720 | tf_op jit(solution)/shard_map/psum | solution.py:74
  95.0 515.2 %all-gather.5.cloned.1.call-start = ((), (), s32[]{:S(2)}) async-start(), calls=%async_computation.5 | async-start | bytes 5898240 | tf_op jit(solution)/shard_map/all_gather | solution.py:103
  442.1 7.8 %copy-start.3 = (bf16[1,6144,256]{2,1,0:T(8,128)(2,1)S(1)}, bf16[1,6144,256]{2,1,0:T(8,128)(2,1)}, u32[]{:S(2)}) copy-start(bf16[1,6144,256]{2,1,0:T(8,128)(2,1)} %param.13) | copy-start | bytes 9437188
  458.9 46.7 %copy-start.1 = (s32[1,128]{1,0:T(1,128)S(1)}, s32[1,128]{1,0:T(1,128)}, u32[]{:S(2)}) copy-start(s32[1,128]{1,0:T(1,128)} %param.11) | copy-start | bytes 1540
  459.5 54.7 %all-to-all-start.2 = ((bf16[32,1,40]{2,1,0:T(2,128)(2,1)}), bf16[32,1,40]{2,1,0:T(2,128)(2,1)S(1)}, u32[]{:S(2)}, u32[]{:S(2)}) async-start(bf16[32,1,40]{2,1,0:T(2,128)(2,1)} %copy.22), calls=%async_computation.2 | async-start | bytes 32768 | tf_op jit(solution)/shard_map/all_to_all | solution.py:63
  514.8 12.4 %all-to-all-start.1 = ((s32[32,1,40]{2,1,0:T(1,128)}), s32[32,1,40]{2,1,0:T(1,128)S(1)}, u32[]{:S(2)}, u32[]{:S(2)}) async-start(s32[32,1,40]{2,1,0:T(1,128)} %bitcast.13), calls=%async_computation.1 | async-start | bytes 32768 | tf_op jit(solution)/shard_map/all_to_all | solution.py:64
Sparse Core Ops, SparseCore 0:
  9.9 31.1 all-gather.2
  95.1 68.1 all-reduce.1
  459.0 81.5 all-gather.4
where the time goes:
time: 627 us; the launch traced here: 626 us
  waiting for transfers between devices  391 us (62%)
  blocking collectives  76.6 us (12%)
  starting transfers between devices  68.9 us (11%)
  local copies, waits for them, and re-layouts  32.9 us (5%)
  matrix products  31.6 us (5%)
  between operations  14 us (2%)
  other arithmetic  10.6 us (2%)
    all_to_all x1, waiting for transfers between devices, body(): lax.all_to_all(replicate_rows(x_send, group_size), 'ep', split_axis=0, co...  347 us
    psum x1, blocking collectives, body(): norm_sq = lax.psum(partial_norms, ('ep', 'tp'))  76.6 us
    all_to_all x1, starting transfers between devices, body(): lax.all_to_all(gate_send, 'ep', split_axis=0, concat_axis=0, tiled=True)  46 us
    all_to_all x1, waiting for transfers between devices, body(): lax.all_to_all(replicate_rows(c_send, group_size), 'ep', split_axis=0, co...  18.9 us
    gather x1, local copies, waits for them, and re-layouts, body(): x_send = token_full[token_of] * keep_mask[..., None]  13 us
  transfers between devices with their start and end apart: 7, of which 5 were waited for; matrix products, arithmetic and copies ran while one was open for 9% of the time, Pallas kernels for 0%

commit v1 on v0

v1 whole, which is shorter than its diff:
```python
import jax
import jax.numpy as jnp
from jax import lax
from jax.experimental import pallas as pl
from jax.experimental.pallas import tpu as pltpu
from jax.sharding import PartitionSpec as P

D = 6144
FF = 8192
CAP = 40
CLIP_SCALE = 0.6

NX = 4
NZ = 8
TP = 8
TOK = 128
SH = 768
UN = 256
CH = NX * CAP
SLOTS = NZ * CH
PAIR = 2 * CH
ORDER = (0, 1, 7, 2, 6, 3, 5, 4)

F32 = jnp.float32
BF16 = jnp.bfloat16
MESH = pl.DeviceIdType.MESH


def kernel(
    tok, cot, meta, wg_hbm, wu_hbm, out_hbm, ratio,
    tokraw, cotraw, metaraw, sel, xblk, cblk, rowblk, rowmeta,
    xf, cf, hf, wg, wu, accg, accu, outv,
    gcs, ghs, gcr, ghr, cold, colg, nz, nx, nt,
    wsem, lsem, osem,
    xs_s, xs_r, zs_s, zs_r, ys_s, ys_r, y2_s, y2_r, sb_s, sb_r,
    hy_s, hy_r, h2_s, h2_r, hb_s, hb_r, gs_s, gs_r, nz_s, nz_r, nx_s, nx_r, nt_s, nt_r,
):
    ep = lax.axis_index("ep")
    tp = lax.axis_index("tp")
    x, z = ep // NZ, ep % NZ
    y, core = tp // 2, tp % 2
    sib = y * 2 + (1 - core)
    right = ((y + 1) % 4) * 2 + core
    left = ((y + 3) % 4) * 2 + core
    far = ((y + 2) % 4) * 2 + core

    wcopies = [
        pltpu.make_async_copy(wg_hbm, wg, wsem.at[0]),
        pltpu.make_async_copy(wu_hbm, wu, wsem.at[1]),
    ]

    barrier = pltpu.get_barrier_semaphore()
    for d in range(1, NX):
        pl.semaphore_signal(barrier, inc=1, device_id=(((x + d) % NX) * NZ + z, tp), device_id_type=MESH)
    for d in range(1, NZ):
        pl.semaphore_signal(barrier, inc=1, device_id=(x * NZ + (z + d) % NZ, tp), device_id_type=MESH)
    for d in range(1, TP):
        pl.semaphore_signal(barrier, inc=1, device_id=(ep, (tp + d) % TP), device_id_type=MESH)
    pl.semaphore_wait(barrier, NX - 1 + NZ - 1 + TP - 1)

    sends = []

    def send(src, dst, ssem, rsem, dev):
        c = pltpu.make_async_remote_copy(
            src_ref=src, dst_ref=dst, send_sem=ssem, recv_sem=rsem, device_id=dev, device_id_type=MESH
        )
        c.start()
        sends.append(c)
        return c

    def arrived(dst, ssem, rsem):
        pltpu.make_async_remote_copy(
            src_ref=dst, dst_ref=dst, send_sem=ssem, recv_sem=rsem, device_id=(ep, sib), device_id_type=MESH
        ).wait_recv()

    def x_send(kind, src, buf):
        for d in range(1, NX):
            send(src, buf.at[x], xs_s.at[kind, d], xs_r.at[kind, d], (((x + d) % NX) * NZ + z, tp))

    def x_wait(kind, buf):
        for d in range(1, NX):
            arrived(buf.at[(x + NX - d) % NX], xs_s.at[kind, d], xs_r.at[kind, d])

    x_send(0, meta, metaraw)
    x_send(1, tok, tokraw)
    locals_ = [
        pltpu.make_async_copy(meta, metaraw.at[x], lsem.at[0]),
        pltpu.make_async_copy(tok, tokraw.at[x], lsem.at[1]),
        pltpu.make_async_copy(cot, cotraw.at[x], lsem.at[2]),
    ]
    for c in locals_:
        c.start()
    for c in wcopies:
        c.start()
    for c in locals_:
        c.wait()
    x_wait(0, metaraw)

    earlier = (
        lax.broadcasted_iota(jnp.int32, (TOK, TOK), 0) < lax.broadcasted_iota(jnp.int32, (TOK, TOK), 1)
    ).astype(BF16)
    members, gates, names = [], [], []
    for h in range(2):
        expert = (2 * x + h).astype(F32)
        for s in range(NX):
            m = metaraw[s]
            first = (m[0:1] == expert).astype(F32)
            second = (m[1:2] == expert).astype(F32)
            members.append(first + second)
            gates.append(first * m[2:3] + second * m[3:4])
            names.append(m[4:5] + (s * 4 * NZ + z * 4).astype(F32))
    member = jnp.concatenate(members, axis=0)
    rank = jnp.dot(member.astype(BF16), earlier, preferred_element_type=F32)
    rank = jnp.where(member > 0.5, rank, -1000.0)
    slot_iota = lax.broadcasted_iota(jnp.int32, (CH, TOK), 0).astype(F32)
    for h in range(2):
        for s in range(NX):
            place = rank[h * NX + s : h * NX + s + 1] + float(s * CAP)
            sel[h, :, s * TOK : (s + 1) * TOK] = (slot_iota == place).astype(F32).astype(BF16)
        values = jnp.concatenate(
            [
                jnp.concatenate(gates[h * NX : (h + 1) * NX], axis=1),
                jnp.concatenate(names[h * NX : (h + 1) * NX], axis=1),
                jnp.zeros((6, NX * TOK), F32),
            ],
            axis=0,
        )
        rows = lax.dot_general(
            values.astype(BF16), sel[h], (((1,), (1,)), ((), ())), preferred_element_type=F32
        )
        rowblk[h] = jnp.concatenate([rows, jnp.zeros((8, 256 - CH), F32)], axis=1)

    x_wait(1, tokraw)
    x_send(2, cot, cotraw)
    raw = tokraw[...].reshape(NX * TOK, SH)
    for h in range(2):
        xblk[h] = jnp.dot(sel[h], raw, preferred_element_type=F32).astype(BF16)

    def rows_of(k):
        return pl.ds(k * CH, CH)

    mine = z // 4
    for k in range(1, NZ):
        zd = (z + NZ - ORDER[k]) % NZ
        send(xblk.at[zd // 4], xf.at[tp, rows_of(k)], zs_s.at[0, k], zs_r.at[0, k], (x * NZ + zd, tp))
    for k in range(1, NZ):
        zd = (z + NZ - ORDER[k]) % NZ
        send(rowblk.at[zd // 4], rowmeta.at[z], zs_s.at[1, k], zs_r.at[1, k], (x * NZ + zd, tp))
    own = pltpu.make_async_copy(xblk.at[mine], xf.at[tp, rows_of(0)], lsem.at[3])
    own.start()
    rowmeta[z] = rowblk[mine]
    own.wait()

    def start_c():
        for k in range(1, NZ):
            zd = (z + NZ - ORDER[k]) % NZ
            send(cblk.at[zd // 4], cf.at[rows_of(k)], zs_s.at[2, k], zs_r.at[2, k], (x * NZ + zd, tp))

    def build_c():
        x_wait(2, cotraw)
        craw = cotraw[...].reshape(NX * TOK, SH)
        for h in range(2):
            cblk[h] = jnp.dot(sel[h], craw, preferred_element_type=F32).astype(BF16)
        cf[rows_of(0)] = cblk[mine]

    def spread(buf, rows, k, sy_s, sy_r, b_s, b_r):
        send(buf.at[tp, rows], buf.at[tp, rows], sy_s.at[0, k], sy_r.at[0, k], (ep, right))
        send(buf.at[tp, rows], buf.at[tp, rows], sy_s.at[1, k], sy_r.at[1, k], (ep, left))
        send(buf.at[tp, rows], buf.at[tp, rows], b_s.at[0, k], b_r.at[0, k], (ep, sib))

    def pass_on(buf, rows, k, sy_s, sy_r, f_s, f_r, b_s, b_r):
        arrived(buf.at[left, rows], sy_s.at[0, k], sy_r.at[0, k])
        if k % 2 == 0:
            send(buf.at[left, rows], buf.at[left, rows], f_s.at[k], f_r.at[k], (ep, right))
        send(buf.at[left, rows], buf.at[left, rows], b_s.at[1, k], b_r.at[1, k], (ep, sib))
        arrived(buf.at[right, rows], sy_s.at[1, k], sy_r.at[1, k])
        if k % 2 == 1:
            send(buf.at[right, rows], buf.at[right, rows], f_s.at[k], f_r.at[k], (ep, left))
        send(buf.at[right, rows], buf.at[right, rows], b_s.at[2, k], b_r.at[2, k], (ep, sib))

    def last_hop(buf, rows, k, f_s, f_r, b_s, b_r):
        arrived(buf.at[far, rows], f_s.at[k], f_r.at[k])
        send(buf.at[far, rows], buf.at[far, rows], b_s.at[3, k], b_r.at[3, k], (ep, sib))

    def from_sibling(buf, rows, k, b_s, b_r):
        for i, owner in enumerate((tp, left, right, far)):
            other = (owner // 2) * 2 + (1 - core)
            arrived(buf.at[other, rows], b_s.at[i, k], b_r.at[i, k])

    lane_iota = lax.broadcasted_iota(jnp.int32, (CAP, CH), 1)

    def compact(g):
        total = jnp.zeros((CAP, CH), F32)
        for b in range(NX):
            inside = (lane_iota >= b * CAP) & (lane_iota < (b + 1) * CAP)
            total = total + jnp.where(inside, g[b * CAP : (b + 1) * CAP], 0.0)
        return total

    def gram(block, which, k, out_buf, in_buf):
        g = compact(
            lax.dot_general(block, block, (((1,), (1,)), ((), ())), preferred_element_type=F32)
        )
        g = jnp.concatenate([g, jnp.zeros((CAP, 256 - CH), F32)], axis=1)
        owner = (z + ORDER[k]) % NZ
        out_buf[k] = g

        @pl.when(owner != tp)
        def _():
            pltpu.make_async_remote_copy(
                src_ref=out_buf.at[k], dst_ref=in_buf.at[tp], send_sem=gs_s.at[which, k],
                recv_sem=gs_r.at[which, tp], device_id=(ep, owner), device_id_type=MESH,
            ).start()

        @pl.when(owner == tp)
        def _():
            in_buf[tp] = g

    def gram_sent(which, k, out_buf, in_buf):
        owner = (z + ORDER[k]) % NZ

        @pl.when(owner != tp)
        def _():
            pltpu.make_async_remote_copy(
                src_ref=out_buf.at[k], dst_ref=in_buf.at[tp], send_sem=gs_s.at[which, k],
                recv_sem=gs_r.at[which, tp], device_id=(ep, owner), device_id_type=MESH,
            ).wait_send()

    def hidden_pair(p):
        rows = pl.ds(p * PAIR, PAIR)
        accg[...] = jnp.zeros_like(accg)
        accu[...] = jnp.zeros_like(accu)

        @pl.loop(0, TP)
        def _(j):
            depth = pl.ds(pl.multiple_of(j * SH, SH), SH)
            block = xf[j, rows, :]
            accg[...] += jnp.dot(block, wg[0, depth, :], preferred_element_type=F32)
            accu[...] += jnp.dot(block, wu[0, depth, :], preferred_element_type=F32)

        g = accg[...]
        h = (g / (1.0 + jnp.exp(-g)) * accu[...]).astype(BF16)
        hf[tp, rows, :] = h
        spread(hf, rows, p, hy_s, hy_r, hb_s, hb_r)
        for i in range(2):
            gram(h[i * CH : (i + 1) * CH], 1, 2 * p + i, ghs, ghr)

    for s in range(NZ + 5):
        if s < NZ:
            if s > 0:
                arrived(xf.at[tp, rows_of(s)], zs_s.at[0, s], zs_r.at[0, s])
            spread(xf, rows_of(s), s, ys_s, ys_r, sb_s, sb_r)
        if s == 1:
            build_c()
        if s == 4:
            start_c()
        k = s - 1
        if 0 <= k < NZ:
            pass_on(xf, rows_of(k), k, ys_s, ys_r, y2_s, y2_r, sb_s, sb_r)
        k = s - 2
        if 0 <= k < NZ:
            last_hop(xf, rows_of(k), k, y2_s, y2_r, sb_s, sb_r)
        if s >= 5 and s % 2 == 1 and (s - 5) // 2 < 4:
            p = (s - 5) // 2
            pass_on(hf, pl.ds(p * PAIR, PAIR), p, hy_s, hy_r, h2_s, h2_r, hb_s, hb_r)
        if s >= 6 and s % 2 == 0 and (s - 6) // 2 < 4:
            p = (s - 6) // 2
            last_hop(hf, pl.ds(p * PAIR, PAIR), p, h2_s, h2_r, hb_s, hb_r)
        k = s - 3
        if 0 <= k < NZ and k % 2 == 1:
            if k == 1:
                for c in wcopies:
                    c.wait()
            for q in (k - 1, k):
                from_sibling(xf, rows_of(q), q, sb_s, sb_r)
            hidden_pair(k // 2)

    eye = (
        lax.broadcasted_iota(jnp.int32, (CH, CH), 0) == lax.broadcasted_iota(jnp.int32, (CH, CH), 1)
    ).astype(BF16)
    for k in range(NZ):
        srcz = (z + ORDER[k]) % NZ
        if k > 0:
            arrived(cf.at[rows_of(k)], zs_s.at[2, k], zs_r.at[2, k])
            arrived(rowmeta.at[srcz], zs_s.at[1, k], zs_r.at[1, k])
        gram(cf[rows_of(k)], 0, k, gcs, gcr)
        rows = rowmeta[srcz][:, :CH]
        cols = lax.dot_general(eye, rows.astype(BF16), (((1,), (1,)), ((), ())), preferred_element_type=F32)
        colg[rows_of(k)] = cols[:, 0:1]
        cold[rows_of(k)] = cols[:, 1:2]

    for d in range(1, TP):
        j = (tp + d) % TP
        arrived(gcr.at[j], gs_s.at[0, 0], gs_r.at[0, j])
        arrived(ghr.at[j], gs_s.at[1, 0], gs_r.at[1, j])
    csum, hsum = gcr[0], ghr[0]
    for j in range(1, TP):
        csum = csum + gcr[j]
        hsum = hsum + ghr[j]
    rows = rowmeta[tp][:, :CH]
    cols = lax.dot_general(eye, rows.astype(BF16), (((1,), (1,)), ((), ())), preferred_element_type=F32)
    weight = jnp.where(cols[:, 1:2] == rows[1:2], cols[:, 0:1] * rows[0:1], 0.0)
    terms = compact(weight) * hsum[:, :CH] * csum[:, :CH]
    per_slot = jnp.sum(terms, axis=0, keepdims=True)
    belongs = (
        lax.broadcasted_iota(jnp.int32, (128, CH), 0).astype(F32) == rows[1:2]
    ).astype(F32)
    partial = lax.dot_general(
        jnp.broadcast_to(per_slot, (8, CH)), belongs, (((1,), (1,)), ((), ())),
        preferred_element_type=F32, precision=lax.Precision.HIGHEST,
    )

    def exchange(value, buf, count, me, device_of, ssem, rsem):
        buf[me] = value
        for d in range(1, count):
            send(buf.at[me], buf.at[me], ssem.at[d], rsem.at[d], device_of((me + d) % count))
        for d in range(1, count):
            arrived(buf.at[(me + count - d) % count], ssem.at[d], rsem.at[d])
        total = buf[0]
        for j in range(1, count):
            total = total + buf[j]
        return total

    total = exchange(partial, nz, NZ, z, lambda j: (x * NZ + j, tp), nz_s, nz_r)
    total = exchange(total, nx, NX, x, lambda j: (j * NZ + z, tp), nx_s, nx_r)
    total = exchange(total, nt, TP, tp, lambda j: (ep, j), nt_s, nt_r)

    clip_level = CLIP_SCALE * (FF * D) ** 0.5
    norm = jnp.sqrt(total)
    ratio[...] = norm / clip_level
    factor = (clip_level / jnp.maximum(norm, clip_level))[0:1]

    name_iota = lax.broadcasted_iota(jnp.int32, (CH, 128), 1).astype(F32)
    for k in range(NZ):
        hit = jnp.where(name_iota == cold[rows_of(k)], factor, 0.0)
        slot_factor = jnp.sum(hit, axis=1, keepdims=True)
        scale = slot_factor * colg[rows_of(k)]
        cf[rows_of(k)] = (scale * cf[rows_of(k)].astype(F32)).astype(BF16)

    for p in range(4):
        from_sibling(hf, pl.ds(p * PAIR, PAIR), p, hb_s, hb_r)

    @pl.loop(0, TP)
    def _(j):
        block = lax.dot_general(
            hf[j], cf[...], (((0,), (0,)), ((), ())), preferred_element_type=F32
        )
        outv[pl.ds(pl.multiple_of(j * UN, UN), UN), :] = block.astype(BF16)
        piece = pl.ds(pl.multiple_of(j * UN, UN), UN)
        pltpu.make_async_copy(outv.at[piece], out_hbm.at[0, piece], osem.at[j]).start()

    for k in range(NZ):
        gram_sent(0, k, gcs, gcr)
        gram_sent(1, k, ghs, ghr)
    for c in sends:
        c.wait_send()

    @pl.loop(0, TP)
    def _(j):
        piece = pl.ds(pl.multiple_of(j * UN, UN), UN)
        pltpu.make_async_copy(outv.at[piece], out_hbm.at[0, piece], osem.at[j]).wait()


def body(tokens, cotangent, routes, route_gates, example_ids, gate_weight, up_weight):
    meta = jnp.concatenate(
        [
            routes.T.astype(F32),
            route_gates.T.astype(F32),
            example_ids.astype(F32),
            jnp.zeros((3, TOK), F32),
        ],
        axis=0,
    )
    anywhere = pl.BlockSpec(memory_space=pl.ANY)
    dma = pltpu.SemaphoreType.DMA
    vm = pltpu.VMEM
    update, ratio = pl.pallas_call(
        kernel,
        out_shape=(
            jax.ShapeDtypeStruct((1, TP * UN, SH), BF16),
            jax.ShapeDtypeStruct((8, 128), F32),
        ),
        in_specs=[anywhere, anywhere, pl.BlockSpec(memory_space=vm), anywhere, anywhere],
        out_specs=(anywhere, pl.BlockSpec(memory_space=vm)),
        scratch_shapes=[
            vm((NX, TOK, SH), BF16),
            vm((NX, TOK, SH), BF16),
            vm((NX, 8, TOK), F32),
            vm((2, CH, NX * TOK), BF16),
            vm((2, CH, SH), BF16),
            vm((2, CH, SH), BF16),
            vm((2, 8, 256), F32),
            vm((NZ, 8, 256), F32),
            vm((TP, SLOTS, SH), BF16),
            vm((SLOTS, SH), BF16),
            vm((TP, SLOTS, UN), BF16),
            vm((1, D, UN), BF16),
            vm((1, D, UN), BF16),
            vm((PAIR, UN), F32),
            vm((PAIR, UN), F32),
            vm((TP * UN, SH), BF16),
            vm((NZ, CAP, 256), F32),
            vm((NZ, CAP, 256), F32),
            vm((TP, CAP, 256), F32),
            vm((TP, CAP, 256), F32),
            vm((SLOTS, 1), F32),
            vm((SLOTS, 1), F32),
            vm((NZ, 8, 128), F32),
            vm((NX, 8, 128), F32),
            vm((TP, 8, 128), F32),
            dma((2,)),
            dma((4,)),
            dma((TP,)),
            dma((3, NX)), dma((3, NX)),
            dma((3, NZ)), dma((3, NZ)),
            dma((2, NZ)), dma((2, NZ)),
            dma((NZ,)), dma((NZ,)),
            dma((4, NZ)), dma((4, NZ)),
            dma((2, 4)), dma((2, 4)),
            dma((4,)), dma((4,)),
            dma((4, 4)), dma((4, 4)),
            dma((2, NZ)), dma((2, TP)),
            dma((NZ,)), dma((NZ,)),
            dma((NX,)), dma((NX,)),
            dma((TP,)), dma((TP,)),
        ],
        compiler_params=pltpu.CompilerParams(
            collective_id=0, has_side_effects=True, vmem_limit_bytes=58 * 1024 * 1024
        ),
        cost_estimate=pl.CostEstimate(
            flops=12_000_000_000, bytes_accessed=10_000_000, transcendentals=327_680
        ),
        name="moe_clip",
    )(tokens, cotangent, meta, gate_weight, up_weight)
    return (update, ratio[0])


def solution(mesh):
    placed = (
        P("ep", "tp"),
        P("ep", "tp"),
        P("ep", None),
        P("ep", None),
        P("ep", None),
        P("ep", None, "tp"),
        P("ep", None, "tp"),
    )
    return jax.shard_map(
        body, mesh=mesh, in_specs=placed, out_specs=(P("ep", None, "tp"), P()), check_vma=False
    )
```

time: 627 us -> 170 us (0.27)
  waiting for transfers between devices: 391 us -> 0 us
  Pallas kernels: 0 us -> 162 us
  blocking collectives: 76.6 us -> 0 us
  starting transfers between devices: 68.9 us -> 0 us
  matrix products: 31.6 us -> 0 us
  local copies, waits for them, and re-layouts: 32.9 us -> 5.02 us
  between operations: 14 us -> 0.64 us
  other arithmetic: 10.6 us -> 2.66 us
    all_to_all x4 -> x0, waiting for transfers between devices: 381 us -> none  [the longest x1 347 us: body(): lax.all_to_all(replicate_rows(x_send, group_size), 'ep', split_axis=0, co...]
    pallas_call x0 -> x1, Pallas kernels: none -> 162 us  [body(): pl.pallas_call(kernel, out_shape=(jax.ShapeDtypeStruct((1, TP * UN, SH),...]
    psum x1 -> x0, blocking collectives: 76.6 us -> none  [body(): norm_sq = lax.psum(partial_norms, ('ep', 'tp'))]
    all_to_all x4 -> x0, starting transfers between devices: 68.6 us -> none  [the longest x1 46 us: body(): lax.all_to_all(gate_send, 'ep', split_axis=0, concat_axis=0, tiled=True)]
    dot_general x5 -> x0, matrix products: 31.6 us -> none  [the longest x1 9.13 us: body(): jnp.einsum('sh,sd->hd', lax.all_gather(hidden, 'tp', axis=1, tiled=True),...]
    gather x6 -> x0, local copies, waits for them, and re-layouts: 20.5 us -> none  [the longest x1 13 us: body(): x_send = token_full[token_of] * keep_mask[..., None]]
    all_gather x2 -> x0, waiting for transfers between devices: 9.97 us -> none  [the longest x1 9.97 us: body(): token_full = lax.all_gather(tokens, 'tp', axis=1, tiled=True)]
    broadcast_in_dim x4 -> x1, local copies, waits for them, and re-layouts: 9.06 us -> 0.01 us  [body(): jnp.zeros((3, TOK), F32)]
  transfers between devices with their start and end apart: 7 -> 0, of which waited for: 5 -> 0; matrix products, arithmetic and copies ran while one was open for 9% -> 0% of each run, Pallas kernels for 0% -> 0%
where the time goes in v1:
time: 170 us
  Pallas kernels  162 us (95%)
  local copies, waits for them, and re-layouts  5.02 us (3%)
  other arithmetic  2.66 us (2%)
    pallas_call x1, Pallas kernels, body(): pl.pallas_call(kernel, out_shape=(jax.ShapeDtypeStruct((1, TP * UN, SH),...  162 us
    unnamed x1, local copies, waits for them, and re-layouts  3.75 us

profile of v1, /device:TPU:1, one launch (start us, length us, event | category | flops | bytes accessed | tf_op | source)
XLA Modules:
  0.0 170.3 jit_solution(234438917699557515)
XLA Ops:
  0.6 0.7 convert_element_type.19
  1.3 0.1 pad.3.clone
  1.4 0.7 convert_bitcast_fusion.1
  2.0 0.7 convert_bitcast_fusion
  2.7 0.7 maximum_maximum_fusion.meta
  3.4 161.9 %moe_clip.1 = (bf16[1,2048,768]{2,1,0:T(8,128)(2,1)}, f32[8,128]{1,0:T(8,128)}) custom-call(bf16[128,768]{1,0:T(8,128)(2,1)} %tok.1, bf16[128,768]{1,0:T(8,128)(2,1)} %cot.1, f32[8,128]{1,0:T(8,128)} %maximum_maximum_fusion.meta, bf16[1,6144,256]{2,1,0:T(8,128)(2,1)} %wg_hbm.1, bf16[1,6144,256]{2,1,0:T(8,128)(2,1)} %wu_hbm.1), custom_call_target="tpu_custom_call" | custom-call | flops 12000000000 | bytes 10000000 | tf_op jit(solution)/shard_map/moe_clip/pallas_call | solution.py:376
  165.3 1.2 slice_bitcast_fusion
  166.5 3.8 %copy.10 = bf16[1,2048,768]{2,1,0:T(8,128)(2,1)} copy(bf16[1,2048,768]{2,1,0:T(8,128)(2,1)} %get-tuple-element.8) | data formatting | bytes 6291456
  (1 shorter events, 0.0 us)

commit v2 on v1

v2 whole, which is shorter than its diff:
```python
import jax
import jax.numpy as jnp
from jax import lax
from jax.experimental import pallas as pl
from jax.experimental.pallas import tpu as pltpu
from jax.sharding import PartitionSpec as P

D = 6144
FF = 8192
CAP = 40
CLIP_SCALE = 0.6

NX = 4
NZ = 8
TP = 8
TOK = 128
SH = 768
UN = 256
CH = NX * CAP
SLOTS = NZ * CH
PAIR = 2 * CH

F32 = jnp.float32
BF16 = jnp.bfloat16
MESH = pl.DeviceIdType.MESH


def kernel(
    tok_hbm, cot_hbm, routes, gates, ids, wg_hbm, wu_hbm, out_hbm, ratio,
    tok, cot, metaraw, xs, cs, xraw, craw, sel, perm, xblk, cblk, rowblk, rowmeta,
    xf, cf, outs, hf, wg, wu, accg, accu, outv,
    gcs, gcr, hg, wc, cold, colg, nz, nx, nt,
    wsem, lsem, osem,
    xs_s, xs_r, zs_s, zs_r, ys_s, ys_r, y2_s, y2_r, sb_s, sb_r,
    hy_s, hy_r, h2_s, h2_r, hb_s, hb_r, gs_s, gs_r, wc_s, wc_r, nz_s, nz_r, nx_s, nx_r, nt_s, nt_r,
):
    ep = lax.axis_index("ep")
    tp = lax.axis_index("tp")
    x, z = ep // NZ, ep % NZ
    y, core = tp // 2, tp % 2
    sib = y * 2 + (1 - core)
    right = ((y + 1) % 4) * 2 + core
    left = ((y + 3) % 4) * 2 + core
    far = ((y + 2) % 4) * 2 + core
    q, mine = z % 4, z // 4

    tcopy = pltpu.make_async_copy(tok_hbm, tok, lsem.at[0])
    ccopy = pltpu.make_async_copy(cot_hbm, cot, lsem.at[1])
    wcopies = [
        pltpu.make_async_copy(wg_hbm, wg, wsem.at[0]),
        pltpu.make_async_copy(wu_hbm, wu, wsem.at[1]),
    ]
    tcopy.start()
    ccopy.start()

    barrier = pltpu.get_barrier_semaphore()
    for d in range(1, NX):
        pl.semaphore_signal(barrier, inc=1, device_id=(((x + d) % NX) * NZ + z, tp), device_id_type=MESH)
    for d in range(1, NZ):
        pl.semaphore_signal(barrier, inc=1, device_id=(x * NZ + (z + d) % NZ, tp), device_id_type=MESH)
    for d in range(1, TP):
        pl.semaphore_signal(barrier, inc=1, device_id=(ep, (tp + d) % TP), device_id_type=MESH)

    sends = []

    def send(src, dst, ssem, rsem, dev):
        c = pltpu.make_async_remote_copy(
            src_ref=src, dst_ref=dst, send_sem=ssem, recv_sem=rsem, device_id=dev, device_id_type=MESH
        )
        c.start()
        sends.append(c)
        return c

    def arrived(dst, ssem, rsem):
        pltpu.make_async_remote_copy(
            src_ref=dst, dst_ref=dst, send_sem=ssem, recv_sem=rsem, device_id=(ep, sib), device_id_type=MESH
        ).wait_recv()

    earlier = (
        lax.broadcasted_iota(jnp.int32, (TOK, TOK), 0) < lax.broadcasted_iota(jnp.int32, (TOK, TOK), 1)
    ).astype(BF16)
    r = routes[...].astype(F32)
    metaraw[x] = jnp.concatenate(
        [r, gates[...].astype(F32), ids[...].astype(F32), jnp.zeros((3, TOK), F32)], axis=0
    )
    expert_iota = lax.broadcasted_iota(jnp.int32, (8, TOK), 0).astype(F32)
    member = (expert_iota == r[0:1]).astype(F32) + (expert_iota == r[1:2]).astype(F32)
    rank = jnp.dot(member.astype(BF16), earlier, preferred_element_type=F32)
    rank = jnp.where(member > 0.5, rank, -1000.0)
    cap_iota = lax.broadcasted_iota(jnp.int32, (CAP, TOK), 0).astype(F32)
    own_sel = jnp.concatenate(
        [(cap_iota == rank[e : e + 1]).astype(F32) for e in range(8)], axis=0
    ).astype(BF16)
    tcopy.wait()
    xs[...] = jnp.dot(own_sel, tok[...], preferred_element_type=F32).astype(BF16).reshape(NX, 2 * CAP, SH)

    pl.semaphore_wait(barrier, NX - 1 + NZ - 1 + TP - 1)

    def x_send(kind, src, buf):
        for d in range(1, NX):
            xd = (x + d) % NX
            send(src(xd), buf.at[x], xs_s.at[kind, d], xs_r.at[kind, d], (xd * NZ + z, tp))

    def x_wait(kind, buf):
        for d in range(1, NX):
            arrived(buf.at[(x + NX - d) % NX], xs_s.at[kind, d], xs_r.at[kind, d])

    x_send(1, lambda xd: xs.at[xd], xraw)
    x_send(0, lambda xd: metaraw.at[x], metaraw)
    for c in wcopies:
        c.start()
    xraw[x] = xs[x]
    ccopy.wait()
    cs[...] = jnp.dot(own_sel, cot[...], preferred_element_type=F32).astype(BF16).reshape(NX, 2 * CAP, SH)

    craw[x] = cs[x]

    prow = lax.broadcasted_iota(jnp.int32, (CH, NX * 2 * CAP), 0)
    pcol = lax.broadcasted_iota(jnp.int32, (CH, NX * 2 * CAP), 1)
    source = sum(((prow >= b * CAP).astype(jnp.int32) for b in range(1, NX)), jnp.zeros_like(prow))
    for h in range(2):
        perm[h] = (pcol == prow + source * CAP + h * CAP).astype(F32).astype(BF16)

    x_wait(1, xraw)
    x_send(2, lambda xd: cs.at[xd], craw)
    raw = xraw[...].reshape(NX * 2 * CAP, SH)
    for h in range(2):
        xblk[h] = jnp.dot(perm[h], raw, preferred_element_type=F32).astype(BF16)

    def rows_of(k):
        return pl.ds(k * CH, CH)

    low = (q < 2).astype(jnp.int32)
    short = low * (q + 2) + (1 - low) * (5 - q)

    def place(qq, from_left, d):
        lo = (qq < 2).astype(jnp.int32)
        m = lo * (qq + 2) + (1 - lo) * (5 - qq)
        is_long = lo * (1 - from_left) + (1 - lo) * from_left
        within = (d <= m).astype(jnp.int32)
        return is_long * (within * (2 * d - 1) + (1 - within) * (m + d)) + (1 - is_long) * 2 * d

    from_left_at, dist_at, source_at = [0], [0], [z]
    for k in range(1, NZ):
        is_short = (k <= 2 * short).astype(jnp.int32) * (1 - k % 2)
        beyond = (k > 2 * short).astype(jnp.int32)
        d = is_short * (k // 2) + (1 - is_short) * (beyond * (k - short) + (1 - beyond) * ((k + 1) // 2))
        from_left = is_short * low + (1 - is_short) * (1 - low)
        from_left_at.append(from_left)
        dist_at.append(d)
        source_at.append((z + NZ + d * (1 - 2 * from_left)) % NZ)

    def z_copy(kind, src, dst, where, sidx, zd):
        return pltpu.make_async_remote_copy(
            src_ref=src, dst_ref=dst(where), send_sem=zs_s.at[kind, sidx], recv_sem=zs_r.at[kind, where],
            device_id=(x * NZ + zd, tp), device_id_type=MESH,
        )

    def z_starts(kind, blk, dst):
        to_right = (q >= 2).astype(jnp.int32)
        step = to_right * (4 - q) - (1 - to_right) * (q + 1)
        reach = to_right * (4 - q) + (1 - to_right) * (q + 1)
        entry = (1 - to_right) * 3
        return (
            (q < 3, lambda: z_copy(kind, blk.at[mine], dst, place(q + 1, 1, 1), 0, (z + 1) % NZ)),
            (q > 0, lambda: z_copy(kind, blk.at[mine], dst, place(q + 3 - 4, 0, 1), 8, (z + NZ - 1) % NZ)),
            (q >= 0, lambda: z_copy(kind, blk.at[1 - mine], dst, place(entry, to_right, reach), 9, (z + NZ + step) % NZ)),
        )

    def z_forward(kind, buf, k):
        fl, d = from_left_at[k], dist_at[k]
        go = fl * (q < 3).astype(jnp.int32) + (1 - fl) * (q > 0).astype(jnp.int32)
        qn = q + 2 * fl - 1
        return (
            go == 1,
            lambda: z_copy(kind, buf(k), buf, place(qn, fl, d + 1), k, (z + NZ + 2 * fl - 1) % NZ),
        )

    def x_rows(k):
        return xf.at[tp, pl.ds(pl.multiple_of(k * CH, CH), CH)]

    def c_rows(k):
        return cf.at[pl.ds(pl.multiple_of(k * CH, CH), CH)]

    def m_rows(k):
        return rowmeta.at[k]

    def start_if(pair):
        @pl.when(pair[0])
        def _():
            pair[1]().start()

    def sent_if(pair):
        @pl.when(pair[0])
        def _():
            pair[1]().wait_send()

    zsent = []

    def z_go(pair):
        start_if(pair)
        zsent.append(pair)

    for pair in z_starts(0, xblk, x_rows):
        z_go(pair)
    own = pltpu.make_async_copy(xblk.at[mine], xf.at[tp, rows_of(0)], lsem.at[3])
    own.start()

    def spread(buf, rows, k, sy_s, sy_r, b_s, b_r):
        send(buf.at[tp, rows], buf.at[tp, rows], sy_s.at[0, k], sy_r.at[0, k], (ep, right))
        send(buf.at[tp, rows], buf.at[tp, rows], sy_s.at[1, k], sy_r.at[1, k], (ep, left))
        send(buf.at[tp, rows], buf.at[tp, rows], b_s.at[0, k], b_r.at[0, k], (ep, sib))

    def pass_on(buf, rows, k, sy_s, sy_r, f_s, f_r, b_s, b_r):
        arrived(buf.at[left, rows], sy_s.at[0, k], sy_r.at[0, k])
        if k % 2 == 0:
            send(buf.at[left, rows], buf.at[left, rows], f_s.at[k], f_r.at[k], (ep, right))
        send(buf.at[left, rows], buf.at[left, rows], b_s.at[1, k], b_r.at[1, k], (ep, sib))
        arrived(buf.at[right, rows], sy_s.at[1, k], sy_r.at[1, k])
        if k % 2 == 1:
            send(buf.at[right, rows], buf.at[right, rows], f_s.at[k], f_r.at[k], (ep, left))
        send(buf.at[right, rows], buf.at[right, rows], b_s.at[2, k], b_r.at[2, k], (ep, sib))

    def last_hop(buf, rows, k, f_s, f_r, b_s, b_r):
        arrived(buf.at[far, rows], f_s.at[k], f_r.at[k])
        send(buf.at[far, rows], buf.at[far, rows], b_s.at[3, k], b_r.at[3, k], (ep, sib))

    def from_sibling(buf, rows, k, b_s, b_r):
        for i, owner in enumerate((tp, left, right, far)):
            other = (owner // 2) * 2 + (1 - core)
            arrived(buf.at[other, rows], b_s.at[i, k], b_r.at[i, k])

    own.wait()

    x_wait(0, metaraw)
    members, weights, names = [], [], []
    for h in range(2):
        expert = (2 * x + h).astype(F32)
        for s in range(NX):
            m = metaraw[s]
            first = (m[0:1] == expert).astype(F32)
            second = (m[1:2] == expert).astype(F32)
            members.append(first + second)
            weights.append(first * m[2:3] + second * m[3:4])
            names.append(m[4:5] + (s * 4 * NZ + z * 4).astype(F32))
    member = jnp.concatenate(members, axis=0)
    rank = jnp.dot(member.astype(BF16), earlier, preferred_element_type=F32)
    rank = jnp.where(member > 0.5, rank, -1000.0)
    slot_iota = lax.broadcasted_iota(jnp.int32, (CH, TOK), 0).astype(F32)
    for h in range(2):
        for s in range(NX):
            row = rank[h * NX + s : h * NX + s + 1] + float(s * CAP)
            sel[h, :, s * TOK : (s + 1) * TOK] = (slot_iota == row).astype(F32).astype(BF16)
        values = jnp.concatenate(
            [
                jnp.concatenate(weights[h * NX : (h + 1) * NX], axis=1),
                jnp.concatenate(names[h * NX : (h + 1) * NX], axis=1),
                jnp.zeros((6, NX * TOK), F32),
            ],
            axis=0,
        )
        rows = lax.dot_general(
            values.astype(BF16), sel[h], (((1,), (1,)), ((), ())), preferred_element_type=F32
        )
        rowblk[h] = jnp.concatenate([rows, jnp.zeros((8, 256 - CH), F32)], axis=1)
    for pair in z_starts(1, rowblk, m_rows):
        z_go(pair)
    rowmeta[0] = rowblk[mine]

    lane_iota = lax.broadcasted_iota(jnp.int32, (CAP, CH), 1)

    def compact(g):
        total = jnp.zeros((CAP, CH), F32)
        for b in range(NX):
            inside = (lane_iota >= b * CAP) & (lane_iota < (b + 1) * CAP)
            total = total + jnp.where(inside, g[b * CAP : (b + 1) * CAP], 0.0)
        return total

    def gram(block):
        return compact(
            lax.dot_general(block, block, (((1,), (1,)), ((), ())), preferred_element_type=F32)
        )

    def widen(g):
        return jnp.concatenate([g, jnp.zeros((CAP, 256 - CH), F32)], axis=1)

    eye = (
        lax.broadcasted_iota(jnp.int32, (CH, CH), 0) == lax.broadcasted_iota(jnp.int32, (CH, CH), 1)
    ).astype(BF16)

    def gram_copy(k):
        return (
            source_at[k] != tp,
            lambda: pltpu.make_async_remote_copy(
                src_ref=gcs.at[k], dst_ref=gcr.at[tp], send_sem=gs_s.at[k], recv_sem=gs_r.at[tp],
                device_id=(ep, source_at[k]), device_id_type=MESH,
            ),
        )

    def take_c(k):
        if k > 0:
            arrived(cf.at[rows_of(k)], zs_s.at[2, k], zs_r.at[2, k])
            z_go(z_forward(2, c_rows, k))
            arrived(rowmeta.at[k], zs_s.at[1, k], zs_r.at[1, k])
            z_go(z_forward(1, m_rows, k))
        g = widen(gram(cf[rows_of(k)]))
        gcs[k] = g
        start_if(gram_copy(k))

        @pl.when(source_at[k] == tp)
        def _():
            gcr[tp] = g

        rows = rowmeta[k][:, :CH]
        cols = lax.dot_general(eye, rows.astype(BF16), (((1,), (1,)), ((), ())), preferred_element_type=F32)
        colg[rows_of(k)] = cols[:, 0:1]
        cold[rows_of(k)] = cols[:, 1:2]

        @pl.when(source_at[k] == tp)
        def _():
            weight = jnp.where(cols[:, 1:2] == rows[1:2], cols[:, 0:1] * rows[0:1], 0.0)
            wc[tp] = widen(compact(weight))

    def build_c():
        x_wait(2, craw)
        raw = craw[...].reshape(NX * 2 * CAP, SH)
        for h in range(2):
            cblk[h] = jnp.dot(perm[h], raw, preferred_element_type=F32).astype(BF16)
        cf[rows_of(0)] = cblk[mine]

    def hidden_spread(p):
        spread(hf, pl.ds(p * PAIR, PAIR), p, hy_s, hy_r, hb_s, hb_r)

    def hidden_pass(p):
        pass_on(hf, pl.ds(p * PAIR, PAIR), p, hy_s, hy_r, h2_s, h2_r, hb_s, hb_r)

    def hidden_last(p):
        last_hop(hf, pl.ds(p * PAIR, PAIR), p, h2_s, h2_r, hb_s, hb_r)

    def hidden_chunk(k):
        rows = rows_of(k)
        accg[...] = jnp.zeros_like(accg)
        accu[...] = jnp.zeros_like(accu)

        @pl.loop(0, TP)
        def _(j):
            depth = pl.ds(pl.multiple_of(j * SH, SH), SH)
            block = xf[j, rows, :]
            accg[...] += jnp.dot(block, wg[0, depth, :], preferred_element_type=F32)
            accu[...] += jnp.dot(block, wu[0, depth, :], preferred_element_type=F32)

        g = accg[...]
        h = (g / (1.0 + jnp.exp(-g)) * accu[...]).astype(BF16)
        hf[tp, rows, :] = h
        if k == 5 or k == 7:
            hidden_spread(k // 2)
        hg[k] = gram(h)

    def share(k):
        per_slot = jnp.sum(wc[source_at[k]][:, :CH] * hg[k], axis=0, keepdims=True)
        belongs = (
            lax.broadcasted_iota(jnp.int32, (128, CH), 0).astype(F32) == rowmeta[k][1:2, :CH]
        ).astype(F32)
        return lax.dot_general(
            jnp.broadcast_to(per_slot, (8, CH)), belongs, (((1,), (1,)), ((), ())),
            preferred_element_type=F32, precision=lax.Precision.HIGHEST,
        )

    x_events = {0: (1,), 1: (2,), 2: (3,), 3: (4,), 4: (5,), 5: (6,), 6: (7,)}
    c_events = {3: (0,), 4: (1, 2), 5: (3,), 6: (4,), 7: (5,), 8: (6, 7)}
    partial = None
    for s in range(NZ + 3):
        if s == 0:
            spread(xf, rows_of(0), 0, ys_s, ys_r, sb_s, sb_r)
        for k in x_events.get(s, ()):
            arrived(xf.at[tp, rows_of(k)], zs_s.at[0, k], zs_r.at[0, k])
            z_go(z_forward(0, x_rows, k))
            spread(xf, rows_of(k), k, ys_s, ys_r, sb_s, sb_r)
        k = s - 1
        if 0 <= k < NZ:
            pass_on(xf, rows_of(k), k, ys_s, ys_r, y2_s, y2_r, sb_s, sb_r)
        if s == 1:
            build_c()
        if s == 2:
            for pair in z_starts(2, cblk, c_rows):
                z_go(pair)
        k = s - 2
        if 0 <= k < NZ:
            last_hop(xf, rows_of(k), k, y2_s, y2_r, sb_s, sb_r)
        if s == NZ:
            for p in range(2):
                hidden_spread(p)
        for k in c_events.get(s, ()):
            take_c(k)
        if s == 9:
            for d in range(1, TP):
                j = (tp + d) % TP
                arrived(gcr.at[j], gs_s.at[0], gs_r.at[j])
            csum = gcr[0]
            for j in range(1, TP):
                csum = csum + gcr[j]
            wc[tp] = wc[tp] * csum
            for d in range(1, TP):
                send(wc.at[tp], wc.at[tp], wc_s.at[d], wc_r.at[d], (ep, (tp + d) % TP))
        if s == 10:
            for d in range(1, TP):
                arrived(wc.at[(tp + TP - d) % TP], wc_s.at[d], wc_r.at[d])
            partial = share(0)
            for k in range(1, 7):
                partial = partial + share(k)
        k = s - 3
        if 0 <= k < NZ:
            if k == 0:
                for c in wcopies:
                    c.wait()
            from_sibling(xf, rows_of(k), k, sb_s, sb_r)
            hidden_chunk(k)

    partial = partial + share(7)

    def exchange_start(value, buf, count, me, device_of, ssem, rsem):
        buf[me] = value
        for d in range(1, count):
            send(buf.at[me], buf.at[me], ssem.at[d], rsem.at[d], device_of((me + d) % count))

    def exchange_end(buf, count, me, ssem, rsem):
        for d in range(1, count):
            arrived(buf.at[(me + count - d) % count], ssem.at[d], rsem.at[d])
        total = buf[0]
        for j in range(1, count):
            total = total + buf[j]
        return total

    exchange_start(partial, nz, NZ, z, lambda j: (x * NZ + j, tp), nz_s, nz_r)
    hidden_pass(0)
    total = exchange_end(nz, NZ, z, nz_s, nz_r)
    exchange_start(total, nx, NX, x, lambda j: (j * NZ + z, tp), nx_s, nx_r)
    hidden_pass(1)
    hidden_last(0)
    total = exchange_end(nx, NX, x, nx_s, nx_r)
    exchange_start(total, nt, TP, tp, lambda j: (ep, j), nt_s, nt_r)
    hidden_pass(2)
    hidden_last(1)
    hidden_pass(3)
    hidden_last(2)
    total = exchange_end(nt, TP, tp, nt_s, nt_r)

    clip_level = CLIP_SCALE * (FF * D) ** 0.5
    norm = jnp.sqrt(total[0:1])
    ratio[...] = norm / clip_level
    factor = clip_level / jnp.maximum(norm, clip_level)

    name_iota = lax.broadcasted_iota(jnp.int32, (CH, 128), 1).astype(F32)
    for k in range(NZ):
        hit = jnp.where(name_iota == cold[rows_of(k)], factor, 0.0)
        slot_factor = jnp.sum(hit, axis=1, keepdims=True)
        scale = slot_factor * colg[rows_of(k)]
        cs_k = (scale * cf[rows_of(k)].astype(F32)).astype(BF16)
        outs[rows_of(k)] = cs_k

    hidden_last(3)
    for p in range(4):
        from_sibling(hf, pl.ds(p * PAIR, PAIR), p, hb_s, hb_r)

    @pl.loop(0, TP)
    def _(j):
        block = lax.dot_general(
            hf[j], outs[...], (((0,), (0,)), ((), ())), preferred_element_type=F32
        )
        piece = pl.ds(pl.multiple_of(j * UN, UN), UN)
        outv[piece, :] = block.astype(BF16)
        pltpu.make_async_copy(outv.at[piece], out_hbm.at[0, piece], osem.at[j]).start()

    for k in range(NZ):
        sent_if(gram_copy(k))
    for pair in zsent:
        sent_if(pair)
    for c in sends:
        c.wait_send()

    @pl.loop(0, TP)
    def _(j):
        piece = pl.ds(pl.multiple_of(j * UN, UN), UN)
        pltpu.make_async_copy(outv.at[piece], out_hbm.at[0, piece], osem.at[j]).wait()


def body(tokens, cotangent, routes, route_gates, example_ids, gate_weight, up_weight):
    anywhere = pl.BlockSpec(memory_space=pl.ANY)
    dma = pltpu.SemaphoreType.DMA
    vm = pltpu.VMEM
    inside = pl.BlockSpec(memory_space=vm)
    update, ratio = pl.pallas_call(
        kernel,
        out_shape=(
            jax.ShapeDtypeStruct((1, TP * UN, SH), BF16),
            jax.ShapeDtypeStruct((1, 128), F32),
        ),
        in_specs=[anywhere, anywhere, inside, inside, inside, anywhere, anywhere],
        out_specs=(anywhere, inside),
        scratch_shapes=[
            vm((TOK, SH), BF16),
            vm((TOK, SH), BF16),
            vm((NX, 8, TOK), F32),
            vm((NX, 2 * CAP, SH), BF16),
            vm((NX, 2 * CAP, SH), BF16),
            vm((NX, 2 * CAP, SH), BF16),
            vm((NX, 2 * CAP, SH), BF16),
            vm((2, CH, NX * TOK), BF16),
            vm((2, CH, NX * 2 * CAP), BF16),
            vm((2, CH, SH), BF16),
            vm((2, CH, SH), BF16),
            vm((2, 8, 256), F32),
            vm((NZ, 8, 256), F32),
            vm((TP, SLOTS, SH), BF16),
            vm((SLOTS, SH), BF16),
            vm((SLOTS, SH), BF16),
            vm((TP, SLOTS, UN), BF16),
            vm((1, D, UN), BF16),
            vm((1, D, UN), BF16),
            vm((CH, UN), F32),
            vm((CH, UN), F32),
            vm((TP * UN, SH), BF16),
            vm((NZ, CAP, 256), F32),
            vm((TP, CAP, 256), F32),
            vm((NZ, CAP, CH), F32),
            vm((TP, CAP, 256), F32),
            vm((SLOTS, 1), F32),
            vm((SLOTS, 1), F32),
            vm((NZ, 8, 128), F32),
            vm((NX, 8, 128), F32),
            vm((TP, 8, 128), F32),
            dma((2,)),
            dma((4,)),
            dma((TP,)),
            dma((3, NX)), dma((3, NX)),
            dma((3, NZ + 2)), dma((3, NZ)),
            dma((2, NZ)), dma((2, NZ)),
            dma((NZ,)), dma((NZ,)),
            dma((4, NZ)), dma((4, NZ)),
            dma((2, 4)), dma((2, 4)),
            dma((4,)), dma((4,)),
            dma((4, 4)), dma((4, 4)),
            dma((NZ,)), dma((TP,)),
            dma((TP,)), dma((TP,)),
            dma((NZ,)), dma((NZ,)),
            dma((NX,)), dma((NX,)),
            dma((TP,)), dma((TP,)),
        ],
        compiler_params=pltpu.CompilerParams(
            collective_id=0, has_side_effects=True, vmem_limit_bytes=58 * 1024 * 1024
        ),
        cost_estimate=pl.CostEstimate(
            flops=12_000_000_000, bytes_accessed=10_000_000, transcendentals=327_680
        ),
        name="moe_clip",
    )(tokens, cotangent, routes.T, route_gates.T, example_ids, gate_weight, up_weight)
    return (update, ratio.reshape(128))


def solution(mesh):
    placed = (
        P("ep", "tp"),
        P("ep", "tp"),
        P("ep", None),
        P("ep", None),
        P("ep", None),
        P("ep", None, "tp"),
        P("ep", None, "tp"),
    )
    return jax.shard_map(
        body, mesh=mesh, in_specs=placed, out_specs=(P("ep", None, "tp"), P()), check_vma=False
    )
```

time: 170 us -> 147 us (0.86)
  Pallas kernels: 162 us -> 142 us
  other arithmetic: 2.66 us -> 0 us
    pallas_call x1, Pallas kernels: 162 us -> 142 us  [body(): pl.pallas_call(kernel, out_shape=(jax.ShapeDtypeStruct((1, TP * UN, SH),...]
    convert_element_type x3 -> x0, other arithmetic: 2 us -> none  [the longest x1 0.68 us: body(): routes.T.astype(F32)]
    unnamed x1 -> x4, local copies, waits for them, and re-layouts: 3.75 us -> 4.27 us
where the time goes in v2:
time: 147 us
  Pallas kernels  142 us (97%)
  local copies, waits for them, and re-layouts  4.27 us (3%)
    pallas_call x1, Pallas kernels, body(): pl.pallas_call(kernel, out_shape=(jax.ShapeDtypeStruct((1, TP * UN, SH),...  142 us
    unnamed x4, local copies, waits for them, and re-layouts  4.27 us

profile of v2, /device:TPU:1, one launch (start us, length us, event | category | flops | bytes accessed | tf_op | source)
XLA Modules:
  0.0 147.0 jit_solution(2785409290653167591)
XLA Ops:
  0.6 142.1 %moe_clip.1 = (bf16[1,2048,768]{2,1,0:T(8,128)(2,1)}, f32[1,128]{1,0:T(1,128)}) custom-call(bf16[128,768]{1,0:T(8,128)(2,1)} %tok_hbm.1, bf16[128,768]{1,0:T(8,128)(2,1)} %cot_hbm.1, s32[2,128]{1,0:T(2,128)} %bitcast.3, bf16[2,128]{1,0:T(2,128)(2,1)} %bitcast.4, s32[1,128]{1,0:T(1,128)} %ids.1, bf16[1,6144,256]{2,1,0:T(8,128)(2,1)} %wg_hbm.1, ...), custom_call_target="tpu_custom_call" | custom-call | flops 12000000000 | bytes 10000000 | tf_op jit(solution)/shard_map/moe_clip/pallas_call | solution.py:492
  142.7 0.0 copy-start
  142.7 3.8 %copy.11 = bf16[1,2048,768]{2,1,0:T(8,128)(2,1)} copy(bf16[1,2048,768]{2,1,0:T(8,128)(2,1)} %get-tuple-element.8) | data formatting | bytes 6291456
  146.5 0.0 copy-done
  146.5 0.5 copy.12
Async XLA Ops:
  142.7 3.8 %copy-start = (f32[1,128]{1,0:T(1,128)S(1)}, f32[1,128]{1,0:T(1,128)}, u32[]{:S(2)}) copy-start(f32[1,128]{1,0:T(1,128)} %get-tuple-element.5) | copy-start | bytes 1540

commit v3 on v2

--- a/solution.py
+++ b/solution.py
@@ -29,10 +29,10 @@
     tok_hbm, cot_hbm, routes, gates, ids, wg_hbm, wu_hbm, out_hbm, ratio,
     tok, cot, metaraw, xs, cs, xraw, craw, sel, perm, xblk, cblk, rowblk, rowmeta,
     xf, cf, outs, hf, wg, wu, accg, accu, outv,
-    gcs, gcr, hg, wc, cold, colg, nz, nx, nt,
+    gcs, gcr, wcs, hg, wc, cold, colg, nz, nx, nt,
     wsem, lsem, osem,
     xs_s, xs_r, zs_s, zs_r, ys_s, ys_r, y2_s, y2_r, sb_s, sb_r,
-    hy_s, hy_r, h2_s, h2_r, hb_s, hb_r, gs_s, gs_r, wc_s, wc_r, nz_s, nz_r, nx_s, nx_r, nt_s, nt_r,
+    hy_s, hy_r, h2_s, h2_r, hb_s, hb_r, gs_s, gs_r, wz_s, wz_r, wc_s, wc_r, wb_s, wb_r, nz_s, nz_r, nx_s, nx_r, nt_s, nt_r,
 ):
     ep = lax.axis_index("ep")
     tp = lax.axis_index("tp")
@@ -288,14 +288,49 @@
         lax.broadcasted_iota(jnp.int32, (CH, CH), 0) == lax.broadcasted_iota(jnp.int32, (CH, CH), 1)
     ).astype(BF16)
 
-    def gram_copy(k):
-        return (
-            source_at[k] != tp,
-            lambda: pltpu.make_async_remote_copy(
-                src_ref=gcs.at[k], dst_ref=gcr.at[tp], send_sem=gs_s.at[k], recv_sem=gs_r.at[tp],
-                device_id=(ep, source_at[k]), device_id_type=MESH,
-            ),
-        )
+    def remote(src, dst, ssem, rsem, dev):
+        return pltpu.make_async_remote_copy(
+            src_ref=src, dst_ref=dst, send_sem=ssem, recv_sem=rsem, device_id=dev, device_id_type=MESH
+        )
+
+    def source_products():
+        for h in range(2):
+            gcs[h] = widen(gram(cblk[h]))
+        z_go((tp != z, lambda: remote(gcs, gcr.at[tp], gs_s.at[0], gs_r.at[tp], (ep, z))))
+
+    def owner_products():
+        @pl.when(tp == z)
+        def _():
+            gcr[z] = gcs[...]
+            for d in range(1, TP):
+                arrived(gcr.at[(tp + d) % TP], gs_s.at[0], gs_r.at[(tp + d) % TP])
+            for h in range(2):
+                rows = rowblk[h][:, :CH]
+                cols = lax.dot_general(
+                    eye, rows.astype(BF16), (((1,), (1,)), ((), ())), preferred_element_type=F32
+                )
+                weight = jnp.where(cols[:, 1:2] == rows[1:2], cols[:, 0:1] * rows[0:1], 0.0)
+                total = gcr[0, h]
+                for j in range(1, TP):
+                    total = total + gcr[j, h]
+                wcs[h] = widen(compact(weight)) * total
+            wc[z] = wcs[mine]
+
+        for d in range(1, NZ):
+            zd = (z + d) % NZ
+            z_go((
+                tp == z,
+                lambda zd=zd, d=d: remote(wcs.at[zd // 4], wc.at[z], wz_s.at[d], wz_r.at[0], (x * NZ + zd, tp)),
+            ))
+
+    def gather_products():
+        @pl.when(tp != z)
+        def _():
+            arrived(wc.at[tp], wz_s.at[1], wz_r.at[0])
+
+        for i in (1, 2, 3):
+            send(wc.at[tp], wc.at[tp], wc_s.at[i], wc_r.at[i], (ep, ((y + i) % 4) * 2 + core))
+        send(wc.at[tp], wc.at[tp], wb_s.at[0], wb_r.at[0], (ep, sib))
 
     def take_c(k):
         if k > 0:
@@ -303,23 +338,11 @@
             z_go(z_forward(2, c_rows, k))
             arrived(rowmeta.at[k], zs_s.at[1, k], zs_r.at[1, k])
             z_go(z_forward(1, m_rows, k))
-        g = widen(gram(cf[rows_of(k)]))
-        gcs[k] = g
-        start_if(gram_copy(k))
-
-        @pl.when(source_at[k] == tp)
-        def _():
-            gcr[tp] = g
-
         rows = rowmeta[k][:, :CH]
         cols = lax.dot_general(eye, rows.astype(BF16), (((1,), (1,)), ((), ())), preferred_element_type=F32)
         colg[rows_of(k)] = cols[:, 0:1]
         cold[rows_of(k)] = cols[:, 1:2]
 
-        @pl.when(source_at[k] == tp)
-        def _():
-            weight = jnp.where(cols[:, 1:2] == rows[1:2], cols[:, 0:1] * rows[0:1], 0.0)
-            wc[tp] = widen(compact(weight))
 
     def build_c():
         x_wait(2, craw)
@@ -356,19 +379,28 @@
             hidden_spread(k // 2)
         hg[k] = gram(h)
 
-    def share(k):
-        per_slot = jnp.sum(wc[source_at[k]][:, :CH] * hg[k], axis=0, keepdims=True)
-        belongs = (
-            lax.broadcasted_iota(jnp.int32, (128, CH), 0).astype(F32) == rowmeta[k][1:2, :CH]
-        ).astype(F32)
-        return lax.dot_general(
-            jnp.broadcast_to(per_slot, (8, CH)), belongs, (((1,), (1,)), ((), ())),
-            preferred_element_type=F32, precision=lax.Precision.HIGHEST,
-        )
+    def shares():
+        terms, named = [], []
+        base = jnp.zeros((NZ, 128), jnp.int32)
+        chunk_iota = lax.broadcasted_iota(jnp.int32, (NZ, 128), 0)
+        for k in range(NZ):
+            terms.append(jnp.sum(wc[source_at[k]][:, :CH] * hg[k], axis=0, keepdims=True))
+            named.append(rowmeta[k][1:2, :CH])
+            base = jnp.where(chunk_iota == k, source_at[k] * 4, base)
+        term = jnp.concatenate(terms, axis=0)
+        name = jnp.concatenate(named, axis=0)
+        first = base[:, 0:1].astype(F32)
+        lanes = lax.broadcasted_iota(jnp.int32, (NZ, 128), 1)
+        total = jnp.zeros((NZ, 128), F32)
+        for xs_ in range(NX):
+            for ex in range(4):
+                number = xs_ * 4 * NZ + ex
+                one = jnp.sum(jnp.where(name == first + float(number), term, 0.0), axis=1, keepdims=True)
+                total = total + jnp.where(lanes == base + number, one, 0.0)
+        return jnp.broadcast_to(jnp.sum(total, axis=0, keepdims=True), (8, 128))
 
     x_events = {0: (1,), 1: (2,), 2: (3,), 3: (4,), 4: (5,), 5: (6,), 6: (7,)}
-    c_events = {3: (0,), 4: (1, 2), 5: (3,), 6: (4,), 7: (5,), 8: (6, 7)}
-    partial = None
+    c_events = {2: (0,), 3: (1,), 4: (2,), 5: (3,), 6: (4,), 7: (5,), 8: (6, 7)}
     for s in range(NZ + 3):
         if s == 0:
             spread(xf, rows_of(0), 0, ys_s, ys_r, sb_s, sb_r)
@@ -379,9 +411,10 @@
         k = s - 1
         if 0 <= k < NZ:
             pass_on(xf, rows_of(k), k, ys_s, ys_r, y2_s, y2_r, sb_s, sb_r)
+        if s == 0:
+            build_c()
+            source_products()
         if s == 1:
-            build_c()
-        if s == 2:
             for pair in z_starts(2, cblk, c_rows):
                 z_go(pair)
         k = s - 2
@@ -392,22 +425,17 @@
                 hidden_spread(p)
         for k in c_events.get(s, ()):
             take_c(k)
-        if s == 9:
-            for d in range(1, TP):
-                j = (tp + d) % TP
-                arrived(gcr.at[j], gs_s.at[0], gs_r.at[j])
-            csum = gcr[0]
-            for j in range(1, TP):
-                csum = csum + gcr[j]
-            wc[tp] = wc[tp] * csum
-            for d in range(1, TP):
-                send(wc.at[tp], wc.at[tp], wc_s.at[d], wc_r.at[d], (ep, (tp + d) % TP))
+        if s == 3:
+            owner_products()
+        if s == 5:
+            gather_products()
+        if s == 7:
+            for i in (1, 2, 3):
+                j = ((y + i) % 4) * 2 + core
+                arrived(wc.at[j], wc_s.at[i], wc_r.at[4 - i])
+                send(wc.at[j], wc.at[j], wb_s.at[i], wb_r.at[4 - i], (ep, sib))
         if s == 10:
-            for d in range(1, TP):
-                arrived(wc.at[(tp + TP - d) % TP], wc_s.at[d], wc_r.at[d])
-            partial = share(0)
-            for k in range(1, 7):
-                partial = partial + share(k)
+            hidden_pass(0)
         k = s - 3
         if 0 <= k < NZ:
             if k == 0:
@@ -416,7 +444,9 @@
             from_sibling(xf, rows_of(k), k, sb_s, sb_r)
             hidden_chunk(k)
 
-    partial = partial + share(7)
+    for i in range(4):
+        arrived(wc.at[((y + i) % 4) * 2 + 1 - core], wb_s.at[i], wb_r.at[(4 - i) % 4])
+    partial = shares()
 
     def exchange_start(value, buf, count, me, device_of, ssem, rsem):
         buf[me] = value
@@ -432,14 +462,13 @@
         return total
 
     exchange_start(partial, nz, NZ, z, lambda j: (x * NZ + j, tp), nz_s, nz_r)
-    hidden_pass(0)
+    hidden_pass(1)
     total = exchange_end(nz, NZ, z, nz_s, nz_r)
     exchange_start(total, nx, NX, x, lambda j: (j * NZ + z, tp), nx_s, nx_r)
-    hidden_pass(1)
     hidden_last(0)
+    hidden_pass(2)
     total = exchange_end(nx, NX, x, nx_s, nx_r)
     exchange_start(total, nt, TP, tp, lambda j: (ep, j), nt_s, nt_r)
-    hidden_pass(2)
     hidden_last(1)
     hidden_pass(3)
     hidden_last(2)
@@ -471,8 +500,6 @@
         outv[piece, :] = block.astype(BF16)
         pltpu.make_async_copy(outv.at[piece], out_hbm.at[0, piece], osem.at[j]).start()
 
-    for k in range(NZ):
-        sent_if(gram_copy(k))
     for pair in zsent:
         sent_if(pair)
     for c in sends:
@@ -520,8 +547,9 @@
             vm((CH, UN), F32),
             vm((CH, UN), F32),
             vm((TP * UN, SH), BF16),
-            vm((NZ, CAP, 256), F32),
-            vm((TP, CAP, 256), F32),
+            vm((2, CAP, 256), F32),
+            vm((TP, 2, CAP, 256), F32),
+            vm((2, CAP, 256), F32),
             vm((NZ, CAP, CH), F32),
             vm((TP, CAP, 256), F32),
             vm((SLOTS, 1), F32),
@@ -540,8 +568,10 @@
             dma((2, 4)), dma((2, 4)),
             dma((4,)), dma((4,)),
             dma((4, 4)), dma((4, 4)),
-            dma((NZ,)), dma((TP,)),
-            dma((TP,)), dma((TP,)),
+            dma((1,)), dma((TP,)),
+            dma((NZ,)), dma((1,)),
+            dma((4,)), dma((4,)),
+            dma((4,)), dma((4,)),
             dma((NZ,)), dma((NZ,)),
             dma((NX,)), dma((NX,)),
             dma((TP,)), dma((TP,)),

time: 147 us -> 138 us (0.939)
  Pallas kernels: 142 us -> 133 us
    pallas_call x1, Pallas kernels: 142 us -> 133 us  [body(): pl.pallas_call(kernel, out_shape=(jax.ShapeDtypeStruct((1, TP * UN, SH),...]
where the time goes in v3:
time: 138 us
  Pallas kernels  133 us (96%)
  local copies, waits for them, and re-layouts  4.27 us (3%)
    pallas_call x1, Pallas kernels, body(): pl.pallas_call(kernel, out_shape=(jax.ShapeDtypeStruct((1, TP * UN, SH),...  133 us
    unnamed x4, local copies, waits for them, and re-layouts  4.27 us

profile of v3, /device:TPU:1, one launch (start us, length us, event | category | flops | bytes accessed | tf_op | source)
XLA Modules:
  0.0 137.5 jit_solution(16048928570123139523)
XLA Ops:
  0.6 132.6 %moe_clip.1 = (bf16[1,2048,768]{2,1,0:T(8,128)(2,1)}, f32[1,128]{1,0:T(1,128)}) custom-call(bf16[128,768]{1,0:T(8,128)(2,1)} %tok_hbm.1, bf16[128,768]{1,0:T(8,128)(2,1)} %cot_hbm.1, s32[2,128]{1,0:T(2,128)} %bitcast.3, bf16[2,128]{1,0:T(2,128)(2,1)} %bitcast.4, s32[1,128]{1,0:T(1,128)} %ids.1, bf16[1,6144,256]{2,1,0:T(8,128)(2,1)} %wg_hbm.1, ...), custom_call_target="tpu_custom_call" | custom-call | flops 12000000000 | bytes 10000000 | tf_op jit(solution)/shard_map/moe_clip/pallas_call | solution.py:519
  133.2 0.0 copy-start
  133.2 3.8 %copy.11 = bf16[1,2048,768]{2,1,0:T(8,128)(2,1)} copy(bf16[1,2048,768]{2,1,0:T(8,128)(2,1)} %get-tuple-element.8) | data formatting | bytes 6291456
  137.0 0.0 copy-done
  137.0 0.5 copy.12
Async XLA Ops:
  133.2 3.8 %copy-start = (f32[1,128]{1,0:T(1,128)S(1)}, f32[1,128]{1,0:T(1,128)}, u32[]{:S(2)}) copy-start(f32[1,128]{1,0:T(1,128)} %get-tuple-element.5) | copy-start | bytes 1540

commit v4 on v3

--- a/solution.py
+++ b/solution.py
@@ -400,7 +400,7 @@
         return jnp.broadcast_to(jnp.sum(total, axis=0, keepdims=True), (8, 128))
 
     x_events = {0: (1,), 1: (2,), 2: (3,), 3: (4,), 4: (5,), 5: (6,), 6: (7,)}
-    c_events = {2: (0,), 3: (1,), 4: (2,), 5: (3,), 6: (4,), 7: (5,), 8: (6, 7)}
+    c_events = {3: (0, 1), 4: (2,), 5: (3,), 6: (4,), 7: (5,), 8: (6,), 9: (7,)}
     for s in range(NZ + 3):
         if s == 0:
             spread(xf, rows_of(0), 0, ys_s, ys_r, sb_s, sb_r)

time: 138 us -> 136 us (0.986)
  Pallas kernels: 133 us -> 131 us
    pallas_call x1, Pallas kernels: 133 us -> 131 us  [body(): pl.pallas_call(kernel, out_shape=(jax.ShapeDtypeStruct((1, TP * UN, SH),...]
where the time goes in v4:
time: 136 us
  Pallas kernels  131 us (96%)
  local copies, waits for them, and re-layouts  4.27 us (3%)
    pallas_call x1, Pallas kernels, body(): pl.pallas_call(kernel, out_shape=(jax.ShapeDtypeStruct((1, TP * UN, SH),...  131 us
    unnamed x4, local copies, waits for them, and re-layouts  4.27 us

profile of v4, /device:TPU:1, one launch (start us, length us, event | category | flops | bytes accessed | tf_op | source)
XLA Modules:
  0.0 136.0 jit_solution(9723004474858648080)
XLA Ops:
  0.6 131.1 %moe_clip.1 = (bf16[1,2048,768]{2,1,0:T(8,128)(2,1)}, f32[1,128]{1,0:T(1,128)}) custom-call(bf16[128,768]{1,0:T(8,128)(2,1)} %tok_hbm.1, bf16[128,768]{1,0:T(8,128)(2,1)} %cot_hbm.1, s32[2,128]{1,0:T(2,128)} %bitcast.3, bf16[2,128]{1,0:T(2,128)(2,1)} %bitcast.4, s32[1,128]{1,0:T(1,128)} %ids.1, bf16[1,6144,256]{2,1,0:T(8,128)(2,1)} %wg_hbm.1, ...), custom_call_target="tpu_custom_call" | custom-call | flops 12000000000 | bytes 10000000 | tf_op jit(solution)/shard_map/moe_clip/pallas_call | solution.py:519
  131.8 0.0 copy-start
  131.8 3.8 %copy.11 = bf16[1,2048,768]{2,1,0:T(8,128)(2,1)} copy(bf16[1,2048,768]{2,1,0:T(8,128)(2,1)} %get-tuple-element.8) | data formatting | bytes 6291456
  135.5 0.0 copy-done
  135.5 0.5 copy.12
Async XLA Ops:
  131.8 3.8 %copy-start = (f32[1,128]{1,0:T(1,128)S(1)}, f32[1,128]{1,0:T(1,128)}, u32[]{:S(2)}) copy-start(f32[1,128]{1,0:T(1,128)} %get-tuple-element.5) | copy-start | bytes 1540
